TPU v7x, 512 devices: a whole 4x4x16 slice. The times are simulated.
512 devices in a mesh: batch: 16 (over y, x), centre: 32 (over z, core).
Axes of the slice: x: 4, y: 4, z: 16, core: 2. Of those that a mesh axis runs over, the one named last changes fastest.
Arguments:
- pool: float32 [4096, 1024], P('batch', 'centre'), may hold values from -4.5 to 4.5
- sample_index: int32 [2048], P('batch'), may hold values from 0 to 255
- targets: float32 [2048, 256], P('batch'), may hold values from -6 to 6
- centres: float32 [8192, 1024], P(('batch', 'centre')), may hold values from -4.5 to 4.5
- coeffs: float32 [8192, 256], P(('batch', 'centre')), may hold values from -6 to 6
- eigvecs: float32 [8192, 1024], P(('batch', 'centre')), may hold values from -0.1875 to 0.1875
- eigscale: float32 [1024], replicated, may hold values from 0.1 to 0.95
Outputs:
- new_coeffs: float32 [8192, 256], P(('batch', 'centre'))
Inputs may be any that keep to these rules, and one draw needn't show every extreme that they name: `sample_index`: each batch row's sample lies in the block of 256 training samples held by its own batch group; the index counts within that block.
All inputs are finite; a program needn't handle non-finite values.
Results may differ from a plain program's by a relative error of at most 0.0003.
Values sent between devices are 32-bit elements; how exact they have to be, the bound alone decides.
No kernel may reach another device: no remote copies, remote signals or barrier semaphores. Data moves between devices by JAX's collectives and lax.ppermute only.
A program may use at most 64 MiB of HBM per device.

v0:
```python
import jax
import jax.numpy as jnp
from jax import lax
from jax.sharding import Mesh
from jax.sharding import PartitionSpec as P

PLANE = "plane"
ORDER = [[2, 12, 0, 14, 1, 5, 3, 7, 10, 4, 8, 6, 9, 13, 11, 15]]
FAR = "z_far"
NEAR = "z_near"
CORE = "core"
NEAR_CORE = ("z_near", "core")
CENTRE = ("z_far", "z_near", "core")
NEAR_ORDER = [[0, 1, 3, 2]]
NEAR_CORE_ORDER = [[2 * near + core for near in NEAR_ORDER[0] for core in range(2)]]
EVERY = ("plane", "z_far", "z_near", "core")


def product(left, right, left_dim, right_dim, precision=lax.Precision.HIGH):
    return lax.dot_general(
        left,
        right,
        (((left_dim,), (right_dim,)), ((), ())),
        precision=precision,
        preferred_element_type=jnp.float32,
    )


def swapped(value):
    return lax.ppermute(value, CORE, [(0, 1), (1, 0)])


def exchanged(blocks, axis, groups=None):
    return lax.all_to_all(
        blocks, axis, split_axis=0, concat_axis=0, axis_index_groups=groups, tiled=True
    )


def to_all(value, axis, groups=None):
    return exchanged(jnp.broadcast_to(value, (lax.axis_size(axis), *value.shape)), axis, groups)


def on_device(pool, sample_index, targets, centres, coeffs, eigvecs, eigscale):
    n_plane = lax.axis_size(PLANE)
    n_near = lax.axis_size(NEAR)
    n_core = lax.axis_size(CORE)
    own, width = centres.shape
    rows = sample_index.shape[0]
    outs = coeffs.shape[1]
    total_centres = own * n_plane * lax.axis_size(CENTRE)
    total_rows = rows * n_plane
    core = lax.axis_index(CORE)
    merged = jnp.concatenate([centres, coeffs, eigvecs], axis=1)
    group = to_all(merged, PLANE, ORDER).reshape(own * n_plane, -1)
    chosen = lax.broadcasted_iota(jnp.int32, (pool.shape[0], rows), 0) == sample_index[None, :]
    picked = product(pool, chosen.astype(jnp.float32), 0, 0, lax.Precision.HIGHEST)
    batch_t = lax.all_gather(picked, CENTRE, axis=0, tiled=True)
    group, batch_t = lax.optimization_barrier((group, batch_t))
    zrows, terms = (group[:, :width], group[:, width:])
    kernel = jnp.exp(product(batch_t, zrows, 0, 1) * (1.0 / jnp.sqrt(jnp.float32(width))))
    tall = rows // (n_near * n_core)
    by_core = kernel.reshape(n_near, n_core, tall, -1)

    def term_sums(by_core, of_core):
        taken = lax.dynamic_index_in_dim(by_core, of_core, 1, keepdims=False)
        return product(taken.reshape(rows // n_core, -1), terms, 1, 0)

    give, kept_rows = lax.optimization_barrier((term_sums(by_core, 1 - core), by_core))
    come, keep = lax.optimization_barrier((swapped(give), term_sums(kept_rows, core)))
    part = come + keep
    near_sum = exchanged(part.reshape(n_near, tall, -1), NEAR, NEAR_ORDER).sum(axis=0)
    own_sum = lax.all_gather(near_sum, FAR, axis=0).sum(axis=0)
    whole = lax.all_gather(
        own_sum, NEAR_CORE, axis_index_groups=NEAR_CORE_ORDER, axis=0, tiled=True
    )
    model_norm = 1.0 / jnp.sqrt(jnp.float32(total_centres))
    residual = whole[:, :outs] * model_norm - targets
    scaled = whole[:, outs:] * eigscale
    weight = kernel - product(scaled, terms[:, outs:], 1, 1)
    change = product(weight, residual, 0, 0)
    change = exchanged(change.reshape(n_plane, own, outs), PLANE, ORDER).sum(axis=0)
    step_size = 0.5 * jnp.sqrt(jnp.float32(total_centres) / jnp.float32(total_rows))
    return coeffs - step_size * model_norm * change


def solution(mesh):
    finer = Mesh(mesh.devices.reshape(16, 4, 4, 2), EVERY)
    placed = (
        P(PLANE, CENTRE),
        P(PLANE),
        P(PLANE, None),
        P(EVERY, None),
        P(EVERY, None),
        P(EVERY, None),
        P(),
    )
    return jax.shard_map(
        on_device, mesh=finer, in_specs=placed, out_specs=P(EVERY, None), check_vma=False
    )
```

profile of v0, /device:TPU:1, one launch (start us, length us, event | category | flops | bytes accessed | tf_op | source)
XLA Modules:
  0.0 117.7 jit_solution(12965106669751825569)
XLA Ops:
  0.0 0.0 copy-start
  0.0 0.9 pad_maximum_fusion
  0.9 1.6 %broadcast_in_dim.2 = f32[16,16,2304]{2,1,0:T(8,128)} broadcast(f32[16,2304]{1,0:T(8,128)S(1)} %pad_maximum_fusion), dimensions={1,2} | broadcast | bytes 2506752 | tf_op jit(solution)/shard_map/broadcast_in_dim | solution.py:40
  2.6 0.0 copy-start.4
  2.6 8.5 %all-to-all-start = ((f32[16,16,2304]{2,1,0:T(8,128)}), f32[16,16,2304]{2,1,0:T(8,128)S(1)}, u32[]{:S(2)}, u32[]{:S(2)}) async-start(f32[16,16,2304]{2,1,0:T(8,128)} %broadcast_in_dim.2), calls=%async_computation | async-start | bytes 4718592 | tf_op jit(solution)/shard_map/all_to_all | solution.py:34
  11.1 0.0 copy-done
  11.1 0.0 copy-done.4
  11.1 0.2 convolution_bitcast_fusion
  11.3 38.7 %all_gather.12 = f32[1024,128]{1,0:T(8,128)S(1)} all-gather(f32[32,128]{1,0:T(8,128)S(1)} %convolution_bitcast_fusion), channel_id=1, replica_groups=mesh['plane'=16,'z_far'=4,'z_near'=4,'core'=2] {'z_far','z_near','core'}, dimensions={0}, use_global_device_ids=true | all-gather | bytes 540672 | tf_op jit(solution)/shard_map/all_gather | solution.py:57
  50.0 0.0 all-to-all-done
  50.0 0.6 fusion.4
  50.6 0.5 fusion.2
  51.1 2.1 %collective-permute-start = (f32[64,1280]{1,0:T(8,128)S(1)}, f32[64,1280]{1,0:T(8,128)S(1)}, u32[]{:S(2)}, u32[]{:S(2)}) collective-permute-start(f32[64,1280]{1,0:T(8,128)S(1)} %fusion.2), channel_id=1, source_target_pairs={{0,1},{1,0},{2,3},{3,2},{4,5},{5,4},{6,7},{7,6},{8,9},{9,8},{10,11... | collective-permute-start | bytes 983048 | tf_op jit(solution)/shard_map/ppermute | solution.py:30
  53.2 0.0 copy-start.3
  53.3 0.5 fusion
  53.8 0.9 collective-permute-done
  54.7 0.0 copy-start.1
  54.7 12.1 %all_to_all.15 = f32[4,16,1280]{2,1,0:T(8,128)S(1)} all-to-all(f32[4,16,1280]{2,1,0:T(8,128)S(1)} %bitcast.19), channel_id=1, replica_groups={{0,2,6,4},{1,3,7,5},{8,10,14,12},{9,11,15,13},{16,18,22,20},{17,19,23,2..., dimensions={0} | all-to-all | bytes 655360 | tf_op jit(solution)/shard_map/all_to_all | solution.py:34
  66.8 0.0 copy-start.2
  66.8 17.7 %all-gather = f32[64,1280]{1,0:T(8,128)S(1)} all-gather(f32[16,1280]{1,0:T(8,128)S(1)} %reduce_sum.27), channel_id=2, replica_groups=mesh['plane'=16,'z_far'=4,'z_near'=4,'core'=2] {'z_far'}, dimensions={0}, use_global_device_ids=true | all-gather | bytes 409600 | tf_op jit(solution)/shard_map/all_gather | solution.py:72
  84.5 17.0 %all_gather.15 = f32[128,1280]{1,0:T(8,128)S(1)} all-gather(f32[16,1280]{1,0:T(8,128)S(1)} %reduce_sum.28), channel_id=1, replica_groups={{0,1,2,3,6,7,4,5},{8,9,10,11,14,15,12,13},{16,17,18,19,22,23,20,21},{24..., dimensions={0}, use_global_device_ids=true | all-gather | bytes 737280 | tf_op jit(solution)/shard_map/all_gather | solution.py:73
  101.5 0.0 copy-done.3
  101.5 0.7 convolution_subtract_fusion
  102.1 0.0 copy-done.1
  102.1 0.3 fusion.9
  102.4 14.6 %all_to_all.16 = f32[16,16,256]{2,1,0:T(8,128)S(1)} all-to-all(f32[16,16,256]{2,1,0:T(8,128)S(1)} %bitcast.22), channel_id=1, replica_groups={{64,384,0,448,32,160,96,224,320,128,256,192,288,416,352,480},{65,385,1,..., dimensions={0} | all-to-all | bytes 524288 | tf_op jit(solution)/shard_map/all_to_all | solution.py:34
  117.1 0.0 copy-done.2
  117.1 0.6 multiply_subtract_fusion
  (6 shorter events, 0.1 us)
Async XLA Ops:
  0.0 11.1 %copy-start = (f32[256,32]{0,1:T(8,128)S(1)}, f32[256,32]{0,1:T(8,128)}, u32[]{:S(2)}) copy-start(f32[256,32]{0,1:T(8,128)} %param.7) | copy-start | bytes 98308
  2.6 8.6 %copy-start.4 = (s32[128]{0:T(128)S(1)}, s32[128]{0:T(128)}, u32[]{:S(2)}) copy-start(s32[128]{0:T(128)} %param.8) | copy-start | bytes 1540
  2.6 47.5 %all-to-all-start = ((f32[16,16,2304]{2,1,0:T(8,128)}), f32[16,16,2304]{2,1,0:T(8,128)S(1)}, u32[]{:S(2)}, u32[]{:S(2)}) async-start(f32[16,16,2304]{2,1,0:T(8,128)} %broadcast_in_dim.2), calls=%async_computation | async-start | bytes 4718592 | tf_op jit(solution)/shard_map/all_to_all | solution.py:34
  51.1 3.5 %collective-permute-start = (f32[64,1280]{1,0:T(8,128)S(1)}, f32[64,1280]{1,0:T(8,128)S(1)}, u32[]{:S(2)}, u32[]{:S(2)}) collective-permute-start(f32[64,1280]{1,0:T(8,128)S(1)} %fusion.2), channel_id=1, source_target_pairs={{0,1},{1,0},{2,3},{3,2},{4,5},{5,4},{6,7},{7,6},{8,9},{9,8},{10,11... | collective-permute-start | bytes 983048 | tf_op jit(solution)/shard_map/ppermute | solution.py:30
  53.2 48.2 %copy-start.3 = (f32[1024]{0:T(1024)S(1)}, f32[1024]{0:T(1024)}, u32[]{:S(2)}) copy-start(f32[1024]{0:T(1024)} %param.13) | copy-start | bytes 12292
  54.7 47.4 %copy-start.1 = (f32[128,256]{1,0:T(8,128)S(1)}, f32[128,256]{1,0:T(8,128)}, u32[]{:S(2)}) copy-start(f32[128,256]{1,0:T(8,128)} %param.9) | copy-start | bytes 393220
  66.8 50.3 %copy-start.2 = (f32[16,256]{1,0:T(8,128)S(1)}, f32[16,256]{1,0:T(8,128)}, u32[]{:S(2)}) copy-start(f32[16,256]{1,0:T(8,128)} %param.11) | copy-start | bytes 49156
where the time goes:
time: 118 us
  blocking collectives  100 us (85%)
  starting transfers between devices  10.6 us (9%)
  matrix products  2.72 us (2%)
  local copies, waits for them, and re-layouts  1.7 us (1%)
  other arithmetic  1.61 us (1%)
    all_gather x1, blocking collectives, on_device(): batch_t = lax.all_gather(picked, CENTRE, axis=0, tiled=True)  38.7 us
    all_to_all x2, blocking collectives, exchanged(): lax.all_to_all(blocks, axis, split_axis=0, concat_axis=0, axis_index_grou...  26.7 us
    all_gather x1, blocking collectives, on_device(): own_sum = lax.all_gather(near_sum, FAR, axis=0).sum(axis=0)  17.7 us
    all_gather x1, blocking collectives, on_device(): lax.all_gather(own_sum, NEAR_CORE, axis_index_groups=NEAR_CORE_ORDER, axi...  17 us
    all_to_all x1, starting transfers between devices, exchanged(): lax.all_to_all(blocks, axis, split_axis=0, concat_axis=0, axis_index_grou...  8.54 us
    dot_general x6, matrix products, product(): lax.dot_general(left, right, (((left_dim,), (right_dim,)), ((), ())), pre...  2.72 us
  transfers between devices with their start and end apart: 2, of which 1 were waited for; matrix products, arithmetic and copies ran while one was open for 1% of the time, Pallas kernels for 0%

commit v1 on v0

--- a/solution.py
+++ b/solution.py
@@ -54,7 +54,9 @@
     group = to_all(merged, PLANE, ORDER).reshape(own * n_plane, -1)
     chosen = lax.broadcasted_iota(jnp.int32, (pool.shape[0], rows), 0) == sample_index[None, :]
     picked = product(pool, chosen.astype(jnp.float32), 0, 0, lax.Precision.HIGHEST)
-    batch_t = lax.all_gather(picked, CENTRE, axis=0, tiled=True)
+    batch_t = jnp.concatenate(
+        lax.all_to_all(jnp.stack([picked] * lax.axis_size(CENTRE)), CENTRE, 0, 0), axis=0
+    )
     group, batch_t = lax.optimization_barrier((group, batch_t))
     zrows, terms = (group[:, :width], group[:, width:])
     kernel = jnp.exp(product(batch_t, zrows, 0, 1) * (1.0 / jnp.sqrt(jnp.float32(width))))

time: 118 us -> 165 us (1.40)
  waiting for transfers between devices: 0.91 us -> 62.9 us
  blocking collectives: 100 us -> 66 us
  starting transfers between devices: 10.6 us -> 27.6 us
    all_gather x1 -> x0, blocking collectives: 38.7 us -> none  [on_device(): batch_t = lax.all_gather(picked, CENTRE, axis=0, tiled=True)]
    all_to_all x0 -> x1, waiting for transfers between devices: none -> 32.6 us  [on_device(): lax.all_to_all(jnp.stack([picked] * lax.axis_size(CENTRE)), CENTRE, 0, 0)]
    all_to_all x1, waiting for transfers between devices: 0.01 us -> 29.6 us  [exchanged(): lax.all_to_all(blocks, axis, split_axis=0, concat_axis=0, axis_index_grou...]
    all_to_all x0 -> x1, starting transfers between devices: none -> 16.7 us  [on_device(): lax.all_to_all(jnp.stack([picked] * lax.axis_size(CENTRE)), CENTRE, 0, 0)]
    all_gather x1, blocking collectives: 17 us -> 20.9 us  [on_device(): lax.all_gather(own_sum, NEAR_CORE, axis_index_groups=NEAR_CORE_ORDER, axi...]
  transfers between devices with their start and end apart: 2 -> 3, of which waited for: 1 -> 3; matrix products, arithmetic and copies ran while one was open for 1% -> 1% of each run, Pallas kernels for 0% -> 0%
where the time goes in v1:
time: 165 us
  blocking collectives  66 us (40%)
  waiting for transfers between devices  62.9 us (38%)
  starting transfers between devices  27.6 us (17%)
  matrix products  3.37 us (2%)
  local copies, waits for them, and re-layouts  3.3 us (2%)
    all_to_all x1, waiting for transfers between devices, on_device(): lax.all_to_all(jnp.stack([picked] * lax.axis_size(CENTRE)), CENTRE, 0, 0)  32.6 us
    all_to_all x1, waiting for transfers between devices, exchanged(): lax.all_to_all(blocks, axis, split_axis=0, concat_axis=0, axis_index_grou...  29.6 us
    all_to_all x2, blocking collectives, exchanged(): lax.all_to_all(blocks, axis, split_axis=0, concat_axis=0, axis_index_grou...  27.2 us
    all_gather x1, blocking collectives, on_device(): lax.all_gather(own_sum, NEAR_CORE, axis_index_groups=NEAR_CORE_ORDER, axi...  20.9 us
    all_gather x1, blocking collectives, on_device(): own_sum = lax.all_gather(near_sum, FAR, axis=0).sum(axis=0)  18 us
    all_to_all x1, starting transfers between devices, on_device(): lax.all_to_all(jnp.stack([picked] * lax.axis_size(CENTRE)), CENTRE, 0, 0)  16.7 us
    all_to_all x1, starting transfers between devices, exchanged(): lax.all_to_all(blocks, axis, split_axis=0, concat_axis=0, axis_index_grou...  7.58 us
    dot_general x6, matrix products, product(): lax.dot_general(left, right, (((left_dim,), (right_dim,)), ((), ())), pre...  3.37 us
  transfers between devices with their start and end apart: 3, of which 3 were waited for; matrix products, arithmetic and copies ran while one was open for 1% of the time, Pallas kernels for 0%

profile of v1, /device:TPU:1, one launch (start us, length us, event | category | flops | bytes accessed | tf_op | source)
XLA Modules:
  0.0 164.9 jit_solution(1047168423429885675)
XLA Ops:
  0.0 0.0 copy-start
  0.0 0.8 copy-done
  0.8 0.8 convolution_bitcast_fusion
  1.6 0.9 stack.2
  2.4 16.7 %all-to-all-start.1 = ((f32[32,32,128]{2,1,0:T(8,128)}), f32[32,32,128]{2,1,0:T(8,128)S(1)}, u32[]{:S(2)}, u32[]{:S(2)}) async-start(f32[32,32,128]{2,1,0:T(8,128)} %stack.2), calls=%async_computation.1 | async-start | bytes 1048576 | tf_op jit(solution)/shard_map/all_to_all | solution.py:58
  19.2 0.9 pad_maximum_fusion
  20.1 32.6 %all-to-all-done.1 = f32[32,32,128]{2,1,0:T(8,128)S(1)} async-done(((f32[32,32,128]{2,1,0:T(8,128)}), f32[32,32,128]{2,1,0:T(8,128)S(1)}, u32[]{:S(2)}, u32[]{:S(2)}) %all-to-all-start.1) | async-done | bytes 524320 | tf_op jit(solution)/shard_map/all_to_all | solution.py:58
  52.7 1.6 broadcast_in_dim.2
  54.3 7.6 %all-to-all-start = ((f32[16,16,2304]{2,1,0:T(8,128)}), f32[16,16,2304]{2,1,0:T(8,128)S(1)}, u32[]{:S(2)}, u32[]{:S(2)}) async-start(f32[16,16,2304]{2,1,0:T(8,128)} %broadcast_in_dim.2), calls=%async_computation | async-start | bytes 4718592 | tf_op jit(solution)/shard_map/all_to_all | solution.py:34
  61.9 29.6 %all-to-all-done = f32[16,16,2304]{2,1,0:T(8,128)S(1)} async-done(((f32[16,16,2304]{2,1,0:T(8,128)}), f32[16,16,2304]{2,1,0:T(8,128)S(1)}, u32[]{:S(2)}, u32[]{:S(2)}) %all-to-all-start) | async-done | bytes 2359328 | tf_op jit(solution)/shard_map/all_to_all | solution.py:34
  91.6 0.6 fusion.4
  92.2 0.5 fusion.2
  92.7 3.2 %collective-permute-start = (f32[64,1280]{1,0:T(8,128)S(1)}, f32[64,1280]{1,0:T(8,128)S(1)}, u32[]{:S(2)}, u32[]{:S(2)}) collective-permute-start(f32[64,1280]{1,0:T(8,128)S(1)} %fusion.2), channel_id=1, source_target_pairs={{0,1},{1,0},{2,3},{3,2},{4,5},{5,4},{6,7},{7,6},{8,9},{9,8},{10,11... | collective-permute-start | bytes 983048 | tf_op jit(solution)/shard_map/ppermute | solution.py:30
  96.0 0.0 copy-start.3
  96.0 0.5 fusion
  96.5 0.7 collective-permute-done
  97.2 0.0 copy-start.1
  97.2 15.4 %all_to_all.20 = f32[4,16,1280]{2,1,0:T(8,128)S(1)} all-to-all(f32[4,16,1280]{2,1,0:T(8,128)S(1)} %bitcast.21), channel_id=1, replica_groups={{0,2,6,4},{1,3,7,5},{8,10,14,12},{9,11,15,13},{16,18,22,20},{17,19,23,2..., dimensions={0} | all-to-all | bytes 655360 | tf_op jit(solution)/shard_map/all_to_all | solution.py:34
  112.6 0.0 copy-start.2
  112.6 18.0 %all-gather = f32[64,1280]{1,0:T(8,128)S(1)} all-gather(f32[16,1280]{1,0:T(8,128)S(1)} %reduce_sum.27), channel_id=2, replica_groups=mesh['plane'=16,'z_far'=4,'z_near'=4,'core'=2] {'z_far'}, dimensions={0}, use_global_device_ids=true | all-gather | bytes 409600 | tf_op jit(solution)/shard_map/all_gather | solution.py:74
  130.6 20.9 %all_gather.11 = f32[128,1280]{1,0:T(8,128)S(1)} all-gather(f32[16,1280]{1,0:T(8,128)S(1)} %reduce_sum.28), channel_id=1, replica_groups={{0,1,2,3,6,7,4,5},{8,9,10,11,14,15,12,13},{16,17,18,19,22,23,20,21},{24..., dimensions={0}, use_global_device_ids=true | all-gather | bytes 737280 | tf_op jit(solution)/shard_map/all_gather | solution.py:75
  151.5 0.0 copy-done.3
  151.5 0.7 convolution_subtract_fusion
  152.1 0.0 copy-done.1
  152.2 0.3 fusion.9
  152.5 11.8 %all_to_all.21 = f32[16,16,256]{2,1,0:T(8,128)S(1)} all-to-all(f32[16,16,256]{2,1,0:T(8,128)S(1)} %bitcast.24), channel_id=1, replica_groups={{64,384,0,448,32,160,96,224,320,128,256,192,288,416,352,480},{65,385,1,..., dimensions={0} | all-to-all | bytes 524288 | tf_op jit(solution)/shard_map/all_to_all | solution.py:34
  164.3 0.0 copy-done.2
  164.3 0.6 multiply_subtract_fusion
  (6 shorter events, 0.1 us)
Async XLA Ops:
  0.0 0.8 copy-start
  2.4 50.3 %all-to-all-start.1 = ((f32[32,32,128]{2,1,0:T(8,128)}), f32[32,32,128]{2,1,0:T(8,128)S(1)}, u32[]{:S(2)}, u32[]{:S(2)}) async-start(f32[32,32,128]{2,1,0:T(8,128)} %stack.2), calls=%async_computation.1 | async-start | bytes 1048576 | tf_op jit(solution)/shard_map/all_to_all | solution.py:58
  54.3 37.2 %all-to-all-start = ((f32[16,16,2304]{2,1,0:T(8,128)}), f32[16,16,2304]{2,1,0:T(8,128)S(1)}, u32[]{:S(2)}, u32[]{:S(2)}) async-start(f32[16,16,2304]{2,1,0:T(8,128)} %broadcast_in_dim.2), calls=%async_computation | async-start | bytes 4718592 | tf_op jit(solution)/shard_map/all_to_all | solution.py:34
  92.7 4.5 %collective-permute-start = (f32[64,1280]{1,0:T(8,128)S(1)}, f32[64,1280]{1,0:T(8,128)S(1)}, u32[]{:S(2)}, u32[]{:S(2)}) collective-permute-start(f32[64,1280]{1,0:T(8,128)S(1)} %fusion.2), channel_id=1, source_target_pairs={{0,1},{1,0},{2,3},{3,2},{4,5},{5,4},{6,7},{7,6},{8,9},{9,8},{10,11... | collective-permute-start | bytes 983048 | tf_op jit(solution)/shard_map/ppermute | solution.py:30
  96.0 55.5 %copy-start.3 = (f32[1024]{0:T(1024)S(1)}, f32[1024]{0:T(1024)}, u32[]{:S(2)}) copy-start(f32[1024]{0:T(1024)} %param.13) | copy-start | bytes 12292
  97.2 54.9 %copy-start.1 = (f32[128,256]{1,0:T(8,128)S(1)}, f32[128,256]{1,0:T(8,128)}, u32[]{:S(2)}) copy-start(f32[128,256]{1,0:T(8,128)} %param.9) | copy-start | bytes 393220
  112.6 51.7 %copy-start.2 = (f32[16,256]{1,0:T(8,128)S(1)}, f32[16,256]{1,0:T(8,128)}, u32[]{:S(2)}) copy-start(f32[16,256]{1,0:T(8,128)} %param.11) | copy-start | bytes 49156
